TPU v7x, 128 devices: a whole 4x4x4 slice. The times are simulated.
128 devices in a mesh: row: 16 (over y, x), col: 8 (over z, core).
Axes of the slice: x: 4, y: 4, z: 4, core: 2. Of those that a mesh axis runs over, the one named last changes fastest.
Arguments:
- inputs: bfloat16 [1024, 8192], P('col', 'row'), may hold values from -6 to 6
- out_grad: bfloat16 [1024, 8192], P('col', 'row'), may hold values from -1.5 to 1.5
- gate_pre: bfloat16 [1024, 14336], P('row', 'col'), may hold values from -9 to 9
- up_pre: bfloat16 [1024, 14336], P('row', 'col'), may hold values from -6 to 6
- gate_weight: bfloat16 [8192, 14336], P('row', 'col'), may hold values from -0.0625 to 0.0625
- up_weight: bfloat16 [8192, 14336], P('row', 'col'), may hold values from -0.0625 to 0.0625
- down_weight: bfloat16 [14336, 8192], P('col', 'row'), may hold values from -0.046875 to 0.046875
Outputs:
- input_grad: float32 [1024, 8192], P('col', 'row')
- gate_grad: float32 [8192, 14336], P('row', 'col')
- up_grad: float32 [8192, 14336], P('row', 'col')
- down_grad: float32 [14336, 8192], P('col', 'row')
All inputs are finite; a program needn't handle non-finite values.
Results may differ from a plain program's by a relative error of at most 0.0029.
Values may be sent and summed in bfloat16 or wider, within the bound.
A program may use at most 128 MiB of HBM per device.

v0:
```python
import jax
import jax.numpy as jnp
from jax import lax
from jax.sharding import PartitionSpec as P

LEAD_DIMS = (((0,), (0,)), ((), ()))
LAST_DIMS = (((1,), (1,)), ((), ()))


def swiglu_grads(grad_hidden, gate_pre, up_pre):
    gate_val = gate_pre.astype(jnp.float32)
    up_val = up_pre.astype(jnp.float32)
    gate_sig = jax.nn.sigmoid(gate_val)
    hidden = (gate_val * gate_sig * up_val).astype(jnp.bfloat16)
    grad_gate = (grad_hidden * up_val * gate_sig * (1.0 + gate_val * (1.0 - gate_sig))).astype(
        jnp.bfloat16
    )
    grad_up = (grad_hidden * gate_val * gate_sig).astype(jnp.bfloat16)
    return (hidden, grad_gate, grad_up)


def body(inputs, out_grad, gate_pre, up_pre, gate_weight, up_weight, down_weight):
    input_full, grad_full = (
        lax.all_gather(inputs, "col", axis=0, tiled=True),
        lax.all_gather(out_grad, "col", axis=0, tiled=True),
    )
    partial_sum = lax.dot_general(
        grad_full, down_weight, LAST_DIMS, preferred_element_type=jnp.float32
    )
    grad_hidden = lax.psum(partial_sum, "row")
    gate_all, up_all = (
        lax.all_gather(gate_pre, "row", axis=0, tiled=True),
        lax.all_gather(up_pre, "row", axis=0, tiled=True),
    )
    hidden, grad_gate, grad_up = swiglu_grads(grad_hidden, gate_all, up_all)
    total = lax.dot_general(grad_gate, gate_weight, LAST_DIMS, preferred_element_type=jnp.float32)
    input_grad = lax.psum_scatter(
        total + lax.dot_general(grad_up, up_weight, LAST_DIMS, preferred_element_type=jnp.float32),
        "col",
        scatter_dimension=0,
        tiled=True,
    )
    gate_grad = lax.dot_general(
        input_full, grad_gate, LEAD_DIMS, preferred_element_type=jnp.float32
    )
    up_grad = lax.dot_general(input_full, grad_up, LEAD_DIMS, preferred_element_type=jnp.float32)
    down_grad = lax.dot_general(hidden, grad_full, LEAD_DIMS, preferred_element_type=jnp.float32)
    return (input_grad, gate_grad, up_grad, down_grad)


def solution(mesh):
    in_specs = (
        P("col", "row"),
        P("col", "row"),
        P("row", "col"),
        P("row", "col"),
        P("row", "col"),
        P("row", "col"),
        P("col", "row"),
    )
    out_specs = (P("col", "row"), P("row", "col"), P("row", "col"), P("col", "row"))
    return jax.shard_map(body, mesh=mesh, in_specs=in_specs, out_specs=out_specs, check_vma=False)
```

profile of v0, /device:TPU:0, one launch (start us, length us, event | category | flops | bytes accessed | tf_op | source)
XLA Modules:
  0.0 340.9 jit_solution(9743817639233089111)
XLA Ops:
  7.2 0.7 all-gather.5.cloned.1.call-update
  8.0 0.7 all-gather.7.cloned.1.call-update
  8.7 0.0 all-gather.9.cloned.1.call-start
  8.7 0.7 all-gather.9.cloned.1.call-update
  9.4 0.0 all-reduce.2.cloned.1.call-start
  9.4 26.4 %all-gather.5.cloned.1.call-done = bf16[1024,512]{1,0:T(8,128)(2,1)} async-done(((bf16[128,512]{1,0:T(8,128)(2,1)}), bf16[1024,512]{1,0:T(8,128)(2,1)}) %all-gather.5.cloned.1.call-update) | async-done | bytes 1048592 | tf_op jit(solution)/shard_map/all_gather | solution.py:25
  35.8 6.4 %fusion.13 = f32[1024,1792]{1,0:T(8,128)} fusion(bf16[1024,512]{1,0:T(8,128)(2,1)} %all-gather.5.cloned.1.call-done, bf16[1792,512]{1,0:T(8,128)(2,1)S(1)} %copy-done), kind=kOutput, calls=%fused_computation.21 | convolution fusion | flops 1879048192 | bytes 10223616 | tf_op jit(solution)/shard_map/dot_general | solution.py:27
  42.2 0.0 all-gather.11.cloned.1.call-start
  42.2 0.5 all-gather.11.cloned.1.call-update
  42.8 0.0 reduce-scatter.2.cloned.1.call-start
  42.8 44.6 %all-gather.7.cloned.1.call-done = bf16[1024,1792]{1,0:T(8,128)(2,1)} async-done(((bf16[64,1792]{1,0:T(8,128)(2,1)}), bf16[1024,1792]{1,0:T(8,128)(2,1)}) %all-gather.7.cloned.1.call-update) | async-done | bytes 3670032 | tf_op jit(solution)/shard_map/all_gather | solution.py:33
  87.4 50.9 %all-gather.9.cloned.1.call-done = bf16[1024,1792]{1,0:T(8,128)(2,1)} async-done(((bf16[64,1792]{1,0:T(8,128)(2,1)}), bf16[1024,1792]{1,0:T(8,128)(2,1)}) %all-gather.9.cloned.1.call-update) | async-done | bytes 3670032 | tf_op jit(solution)/shard_map/all_gather | solution.py:32
  138.3 133.8 %all-reduce.2.cloned.1.call-done = f32[1024,1792]{1,0:T(8,128)} async-done(((f32[1024,1792]{1,0:T(8,128)}), f32[1024,1792]{1,0:T(8,128)}) %all-reduce.2.cloned.1.call-update) | async-done | bytes 7340048 | tf_op jit(solution)/shard_map/psum | solution.py:30
  272.2 7.1 %fusion.9 = (bf16[1024,1792]{1,0:T(8,128)(2,1)S(1)}, bf16[1024,1792]{1,0:T(8,128)(2,1)S(1)}) fusion(f32[1024,1792]{1,0:T(8,128)} %all-reduce.2.cloned.1.call-done, bf16[1024,1792]{1,0:T(8,128)(2,1)} %all-gather.9.cloned.1.call-done, bf16[1024,1792]{1,0:T(8,128)(2,1)} %all-gather.7.cloned.1.call-done), kind=kLoop, calls=%fused_computation.15 | loop fusion | flops 27525120 | bytes 22020096 | tf_op jit(solution)/shard_map/convert_element_type | solution.py:18
  279.4 2.1 fusion.14
  281.5 1.1 copy-done.1
  282.5 3.5 %convolution_add_fusion = f32[1024,512]{1,0:T(8,128)} fusion(f32[1024,512]{1,0:T(8,128)S(1)} %fusion.14, bf16[1024,1792]{1,0:T(8,128)(2,1)S(1)} %get-tuple-element.8, bf16[512,1792]{1,0:T(8,128)(2,1)S(1)} %copy-done.4), kind=kOutput, calls=%fused_computation.19 | convolution fusion | flops 1879572480 | bytes 9699328 | tf_op jit(solution)/shard_map/dot_general | solution.py:38
  286.0 7.8 %fusion.10 = f32[1792,512]{1,0:T(8,128)} fusion(bf16[1024,512]{1,0:T(8,128)(2,1)S(1)} %copy-done.5, bf16[1024,1792]{1,0:T(8,128)(2,1)} %all-gather.7.cloned.1.call-done, bf16[1024,1792]{1,0:T(8,128)(2,1)} %all-gather.9.cloned.1.call-done), kind=kOutput, calls=%fused_computation.16 | convolution fusion | flops 1893728256 | bytes 12058624 | tf_op jit(solution)/shard_map/dot_general | solution.py:47
  293.9 3.4 all-gather.11.cloned.1.call-done
  297.3 6.3 %convolution_bitcast_fusion.1 = f32[512,1792]{0,1:T(8,128)} fusion(bf16[1024,1792]{1,0:T(8,128)(2,1)} %copy-done.2, bf16[1024,512]{1,0:T(8,128)(2,1)} %all-gather.11.cloned.1.call-done), kind=kOutput, calls=%fused_computation.18 | convolution fusion | flops 1879048192 | bytes 8388608 | tf_op jit(solution)/shard_map/dot_general | solution.py:43
  303.5 5.2 %copy.11 = f32[512,1792]{1,0:T(8,128)} copy(f32[512,1792]{0,1:T(8,128)} %convolution_bitcast_fusion.1) | data formatting | bytes 7340032
  308.7 6.0 %convolution_bitcast_fusion = f32[512,1792]{0,1:T(8,128)} fusion(bf16[1024,1792]{1,0:T(8,128)(2,1)} %copy-done.1, bf16[1024,512]{1,0:T(8,128)(2,1)S(1)} %copy-done.6), kind=kOutput, calls=%fused_computation.17 | convolution fusion | flops 1879048192 | bytes 8388608 | tf_op jit(solution)/shard_map/dot_general | solution.py:46
  314.7 5.2 %copy.12 = f32[512,1792]{1,0:T(8,128)} copy(f32[512,1792]{0,1:T(8,128)} %convolution_bitcast_fusion) | data formatting | bytes 7340032
  319.9 14.1 %reduce-scatter.2.cloned.1.call-done = f32[128,512]{1,0:T(8,128)} async-done(((f32[1024,512]{1,0:T(8,128)}), f32[128,512]{1,0:T(8,128)}) %reduce-scatter.2.cloned.1.call-update) | async-done | bytes 262160 | tf_op jit(solution)/shard_map/reduce_scatter | solution.py:37
  (17 shorter events, 0.1 us)
Async XLA Ops:
  7.2 28.6 %copy-start = (bf16[1792,512]{1,0:T(8,128)(2,1)S(1)}, bf16[1792,512]{1,0:T(8,128)(2,1)}, u32[]{:S(2)}) copy-start(bf16[1792,512]{1,0:T(8,128)(2,1)} %param.13) | copy-start | bytes 5505028
  7.2 28.6 %all-gather.5.cloned.1.call-start = ((), (), s32[]{:S(2)}) async-start(), calls=%async_computation.1 | async-start | bytes 1179648 | tf_op jit(solution)/shard_map/all_gather | solution.py:25
  7.9 79.5 %all-gather.7.cloned.1.call-start = ((), (), s32[]{:S(2)}) async-start(), calls=%async_computation.3 | async-start | bytes 3899392 | tf_op jit(solution)/shard_map/all_gather | solution.py:33
  8.7 129.7 %all-gather.9.cloned.1.call-start = ((), (), s32[]{:S(2)}) async-start(), calls=%async_computation.4 | async-start | bytes 3899392 | tf_op jit(solution)/shard_map/all_gather | solution.py:32
  9.4 262.8 %all-reduce.2.cloned.1.call-start = ((), (), s32[]{:S(2)}) async-start(), calls=%async_computation.2 | async-start | bytes 14680064 | tf_op jit(solution)/shard_map/psum | solution.py:30
  42.2 255.1 %all-gather.11.cloned.1.call-start = ((), (), s32[]{:S(2)}) async-start(), calls=%async_computation.6 | async-start | bytes 1179648 | tf_op jit(solution)/shard_map/all_gather | solution.py:24
  42.8 291.3 %reduce-scatter.2.cloned.1.call-start = ((), (), s32[]{:S(2)}) async-start(), calls=%async_computation.5 | async-start | bytes 2359296 | tf_op jit(solution)/shard_map/reduce_scatter | solution.py:37
  272.2 7.2 %copy-start.3 = (bf16[512,1792]{1,0:T(8,128)(2,1)S(1)}, bf16[512,1792]{1,0:T(8,128)(2,1)}, u32[]{:S(2)}) copy-start(bf16[512,1792]{1,0:T(8,128)(2,1)} %param.11) | copy-start | bytes 5505028
  279.3 2.1 copy-start.2
  279.3 3.2 copy-start.1
  279.3 3.2 copy-start.4
  282.5 3.5 %copy-start.5 = (bf16[1024,512]{1,0:T(8,128)(2,1)S(1)}, bf16[1024,512]{1,0:T(8,128)(2,1)}, u32[]{:S(2)}) copy-start(bf16[1024,512]{1,0:T(8,128)(2,1)} %all-gather.5.cloned.1.call-done) | copy-start | bytes 3145732
  303.5 5.2 %copy-start.6 = (bf16[1024,512]{1,0:T(8,128)(2,1)S(1)}, bf16[1024,512]{1,0:T(8,128)(2,1)}, u32[]{:S(2)}) copy-start(bf16[1024,512]{1,0:T(8,128)(2,1)} %all-gather.11.cloned.1.call-done) | copy-start | bytes 3145732
Sparse Core Ops, SparseCore 0:
  9.7 26.0 all-gather.4
  37.9 49.4 all-gather.6
  89.5 48.7 all-gather.8
  141.6 130.4 all-reduce.1
  273.8 23.3 all-gather.10
  300.2 33.7 reduce-scatter.1
where the time goes:
time: 341 us
  waiting for transfers between devices  276 us (81%)
  matrix products  32 us (9%)
  between operations  14.2 us (4%)
  local copies, waits for them, and re-layouts  11.4 us (3%)
  other arithmetic  7.15 us (2%)
    psum x1, waiting for transfers between devices, body(): grad_hidden = lax.psum(partial_sum, 'row')  134 us
    all_gather x1, waiting for transfers between devices, body(): lax.all_gather(gate_pre, 'row', axis=0, tiled=True)  50.9 us
    all_gather x1, waiting for transfers between devices, body(): lax.all_gather(up_pre, 'row', axis=0, tiled=True)  44.6 us
    all_gather x1, waiting for transfers between devices, body(): lax.all_gather(out_grad, 'col', axis=0, tiled=True)  26.4 us
    reduce_scatter x1, waiting for transfers between devices, body(): lax.psum_scatter(total + lax.dot_general(grad_up, up_weight, LAST_DIMS, p...  14.1 us
    unnamed x16, local copies, waits for them, and re-layouts  11.4 us
    dot_general x1, matrix products, body(): lax.dot_general(hidden, grad_full, LEAD_DIMS, preferred_element_type=jnp....  7.83 us
    convert_element_type x1, other arithmetic, swiglu_grads(): grad_up = (grad_hidden * gate_val * gate_sig).astype(jnp.bfloat16)  7.15 us
  transfers between devices with their start and end apart: 6, of which 6 were waited for; matrix products, arithmetic and copies ran while one was open for 15% of the time, Pallas kernels for 0%

commit v1 on v0

--- a/solution.py
+++ b/solution.py
@@ -27,7 +27,11 @@
     partial_sum = lax.dot_general(
         grad_full, down_weight, LAST_DIMS, preferred_element_type=jnp.float32
     )
-    grad_hidden = lax.psum(partial_sum, "row")
+    grad_hidden = partial_sum
+    for hop in (1, 2, 4, 8):
+        grad_hidden = grad_hidden + lax.ppermute(
+            grad_hidden, "row", [(dev, dev ^ hop) for dev in range(16)]
+        )
     gate_all, up_all = (
         lax.all_gather(gate_pre, "row", axis=0, tiled=True),
         lax.all_gather(up_pre, "row", axis=0, tiled=True),

time: 341 us -> 807 us (2.37)
  waiting for transfers between devices: 276 us -> 709 us
  other arithmetic: 7.15 us -> 31.2 us
  starting transfers between devices: 0.23 us -> 9.49 us
    ppermute x0 -> x4, waiting for transfers between devices: none -> 491 us  [body(): lax.ppermute(grad_hidden, 'row', [(dev, dev ^ hop) for dev in range(16)])]
    all_gather x1, waiting for transfers between devices: 50.9 us -> 186 us  [body(): lax.all_gather(gate_pre, 'row', axis=0, tiled=True)]
    psum x1 -> x0, waiting for transfers between devices: 134 us -> none  [body(): grad_hidden = lax.psum(partial_sum, 'row')]
    all_gather x1, waiting for transfers between devices: 44.6 us -> 0.03 us  [body(): lax.all_gather(up_pre, 'row', axis=0, tiled=True)]
    add x0 -> x3, other arithmetic: none -> 22 us  [body(): grad_hidden + lax.ppermute(grad_hidden, 'row', [(dev, dev ^ hop) for dev...]
    reduce_scatter x1, waiting for transfers between devices: 14.1 us -> 2.11 us  [body(): lax.psum_scatter(total + lax.dot_general(grad_up, up_weight, LAST_DIMS, p...]
    ppermute x0 -> x4, starting transfers between devices: none -> 9.1 us  [body(): lax.ppermute(grad_hidden, 'row', [(dev, dev ^ hop) for dev in range(16)])]
  transfers between devices with their start and end apart: 6 -> 9, of which waited for: 6 -> 7; matrix products, arithmetic and copies ran while one was open for 15% -> 7% of each run, Pallas kernels for 0% -> 0%
where the time goes in v1:
time: 807 us
  waiting for transfers between devices  709 us (88%)
  other arithmetic  31.2 us (4%)
  matrix products  29.2 us (4%)
  between operations  15.8 us (2%)
  local copies, waits for them, and re-layouts  12.8 us (2%)
  starting transfers between devices  9.49 us (1%)
    ppermute x4, waiting for transfers between devices, body(): lax.ppermute(grad_hidden, 'row', [(dev, dev ^ hop) for dev in range(16)])  491 us
    all_gather x1, waiting for transfers between devices, body(): lax.all_gather(gate_pre, 'row', axis=0, tiled=True)  186 us
    all_gather x1, waiting for transfers between devices, body(): lax.all_gather(out_grad, 'col', axis=0, tiled=True)  27.8 us
    add x3, other arithmetic, body(): grad_hidden + lax.ppermute(grad_hidden, 'row', [(dev, dev ^ hop) for dev...  22 us
  transfers between devices with their start and end apart: 9, of which 7 were waited for; matrix products, arithmetic and copies ran while one was open for 7% of the time, Pallas kernels for 0%

profile of v1, /device:TPU:0, one launch (start us, length us, event | category | flops | bytes accessed | tf_op | source)
XLA Modules:
  0.0 807.1 jit_solution(17971255257563223520)
XLA Ops:
  8.8 27.8 %all-gather.5.cloned.1.call-done = bf16[1024,512]{1,0:T(8,128)(2,1)} async-done(((bf16[128,512]{1,0:T(8,128)(2,1)}), bf16[1024,512]{1,0:T(8,128)(2,1)}) %all-gather.5.cloned.1.call-update) | async-done | bytes 1048592 | tf_op jit(solution)/shard_map/all_gather | solution.py:25
  36.6 3.3 fusion.14
  40.0 1.5 collective-permute-start
  41.5 1.4 copy-done.2
  42.9 157.4 %collective-permute-done = f32[1024,1792]{1,0:T(8,128)} collective-permute-done((f32[1024,1792]{1,0:T(8,128)S(1)}, f32[1024,1792]{1,0:T(8,128)}, u32[]{:S(2)}, u32[]{:S(2)}) %collective-permute-start) | collective-permute-done | bytes 7340064 | tf_op jit(solution)/shard_map/ppermute | solution.py:32
  200.3 6.1 add.23
  206.4 3.1 collective-permute-start.1
  209.4 158.0 %collective-permute-done.1 = f32[1024,1792]{1,0:T(8,128)} collective-permute-done((f32[1024,1792]{1,0:T(8,128)S(1)}, f32[1024,1792]{1,0:T(8,128)}, u32[]{:S(2)}, u32[]{:S(2)}) %collective-permute-start.1) | collective-permute-done | bytes 7340064 | tf_op jit(solution)/shard_map/ppermute | solution.py:32
  367.4 6.9 add.24
  374.3 1.5 collective-permute-start.2
  375.9 175.6 %collective-permute-done.2 = f32[1024,1792]{1,0:T(8,128)} collective-permute-done((f32[1024,1792]{1,0:T(8,128)}, f32[1024,1792]{1,0:T(8,128)}, u32[]{:S(2)}, u32[]{:S(2)}) %collective-permute-start.2) | collective-permute-done | bytes 7340064 | tf_op jit(solution)/shard_map/ppermute | solution.py:32
  551.5 9.0 %add.25 = f32[1024,1792]{1,0:T(8,128)} add(f32[1024,1792]{1,0:T(8,128)} %add.24, f32[1024,1792]{1,0:T(8,128)} %collective-permute-done.2) | non-fusion elementwise | flops 1835008 | bytes 22020096 | tf_op jit(solution)/shard_map/add | solution.py:32
  560.5 3.0 collective-permute-start.3
  564.4 186.0 %all-gather.9.cloned.1.call-done = bf16[1024,1792]{1,0:T(8,128)(2,1)} async-done(((bf16[64,1792]{1,0:T(8,128)(2,1)}), bf16[1024,1792]{1,0:T(8,128)(2,1)}) %all-gather.9.cloned.1.call-update) | async-done | bytes 3670032 | tf_op jit(solution)/shard_map/all_gather | solution.py:36
  750.4 9.2 %fusion.9 = (bf16[1024,1792]{1,0:T(8,128)(2,1)S(1)}, bf16[1024,1792]{1,0:T(8,128)(2,1)S(1)}) fusion(bf16[1024,1792]{1,0:T(8,128)(2,1)} %all-gather.9.cloned.1.call-done, f32[1024,1792]{1,0:T(8,128)} %add.25, f32[1024,1792]{1,0:T(8,128)} %collective-permute-done.3, bf16[1024,1792]{1,0:T(8,128)(2,1)} %all-gather.7.cloned.1.call-done), kind=kLoop, calls=%fused_computation.15 | loop fusion | flops 29360128 | bytes 29360128 | tf_op jit(solution)/shard_map/convert_element_type | solution.py:18
  759.7 2.1 fusion.15
  761.8 1.0 copy-done.4
  762.8 3.5 fusion.13
  766.3 7.8 fusion.10
  774.6 6.3 convolution_bitcast_fusion.1
  780.8 5.2 copy.11
  786.1 6.2 convolution_bitcast_fusion
  792.2 5.1 copy.12
  797.4 2.1 reduce-scatter.2.cloned.1.call-done
  (29 shorter events, 2.1 us)
Async XLA Ops:
  8.0 28.6 %copy-start = (bf16[1792,512]{1,0:T(8,128)(2,1)S(1)}, bf16[1792,512]{1,0:T(8,128)(2,1)}, u32[]{:S(2)}) copy-start(bf16[1792,512]{1,0:T(8,128)(2,1)} %param.13) | copy-start | bytes 5505028
  8.0 28.6 %all-gather.5.cloned.1.call-start = ((), (), s32[]{:S(2)}) async-start(), calls=%async_computation.1 | async-start | bytes 1179648 | tf_op jit(solution)/shard_map/all_gather | solution.py:25
  8.7 555.7 %all-gather.7.cloned.1.call-start = ((), (), s32[]{:S(2)}) async-start(), calls=%async_computation.2 | async-start | bytes 3899392 | tf_op jit(solution)/shard_map/all_gather | solution.py:37
  40.0 2.9 copy-start.2
  40.0 160.3 %collective-permute-start = (f32[1024,1792]{1,0:T(8,128)S(1)}, f32[1024,1792]{1,0:T(8,128)}, u32[]{:S(2)}, u32[]{:S(2)}) collective-permute-start(f32[1024,1792]{1,0:T(8,128)S(1)} %fusion.14), channel_id=1, source_target_pairs={{0,8},{8,0},{16,24},{24,16},{32,40},{40,32},{48,56},{56,48},{64,72... | collective-permute-start | bytes 22020104 | tf_op jit(solution)/shard_map/ppermute | solution.py:32
  206.4 161.0 %collective-permute-start.1 = (f32[1024,1792]{1,0:T(8,128)S(1)}, f32[1024,1792]{1,0:T(8,128)}, u32[]{:S(2)}, u32[]{:S(2)}) collective-permute-start(f32[1024,1792]{1,0:T(8,128)S(1)} %add.23), channel_id=1, source_target_pairs={{0,16},{8,24},{16,0},{24,8},{32,48},{40,56},{48,32},{56,40},{64,80... | collective-permute-start | bytes 22020104 | tf_op jit(solution)/shard_map/ppermute | solution.py:32
  374.3 177.2 %collective-permute-start.2 = (f32[1024,1792]{1,0:T(8,128)}, f32[1024,1792]{1,0:T(8,128)}, u32[]{:S(2)}, u32[]{:S(2)}) collective-permute-start(f32[1024,1792]{1,0:T(8,128)} %add.24), channel_id=1, source_target_pairs={{0,32},{8,40},{16,48},{24,56},{32,0},{40,8},{48,16},{56,24},{64,96... | collective-permute-start | bytes 22020104 | tf_op jit(solution)/shard_map/ppermute | solution.py:32
  375.8 374.5 %all-gather.9.cloned.1.call-start = ((), (), s32[]{:S(2)}) async-start(), calls=%async_computation.3 | async-start | bytes 3899392 | tf_op jit(solution)/shard_map/all_gather | solution.py:36
  560.5 189.9 %collective-permute-start.3 = (f32[1024,1792]{1,0:T(8,128)}, f32[1024,1792]{1,0:T(8,128)}, u32[]{:S(2)}, u32[]{:S(2)}) collective-permute-start(f32[1024,1792]{1,0:T(8,128)} %add.25), channel_id=1, source_target_pairs={{0,64},{8,72},{16,80},{24,88},{32,96},{40,104},{48,112},{56,120},{... | collective-permute-start | bytes 22020104 | tf_op jit(solution)/shard_map/ppermute | solution.py:32
  563.6 211.0 %all-gather.11.cloned.1.call-start = ((), (), s32[]{:S(2)}) async-start(), calls=%async_computation.5 | async-start | bytes 1179648 | tf_op jit(solution)/shard_map/all_gather | solution.py:24
  564.1 195.5 %copy-start.5 = (bf16[512,1792]{1,0:T(8,128)(2,1)S(1)}, bf16[512,1792]{1,0:T(8,128)(2,1)}, u32[]{:S(2)}) copy-start(bf16[512,1792]{1,0:T(8,128)(2,1)} %param.12) | copy-start | bytes 5505028
  564.1 235.4 %reduce-scatter.2.cloned.1.call-start = ((), (), s32[]{:S(2)}) async-start(), calls=%async_computation.4 | async-start | bytes 2359296 | tf_op jit(solution)/shard_map/reduce_scatter | solution.py:41
  759.7 2.1 copy-start.3
  759.7 3.1 copy-start.4
  759.7 3.1 copy-start.6
  762.8 3.6 copy-start.7
  780.8 5.2 copy-start.8
  786.1 13.4 %copy-start.1 = (bf16[1792,512]{1,0:T(8,128)(2,1)S(1)}, bf16[1792,512]{1,0:T(8,128)(2,1)}, u32[]{:S(2)}) copy-start(bf16[1792,512]{1,0:T(8,128)(2,1)} %param.13) | copy-start | bytes 5505028
Sparse Core Ops, SparseCore 0:
  10.6 26.0 all-gather.4
  766.5 32.9 reduce-scatter.1
Sparse Core Ops, SparseCore 1:
  375.9 63.0 all-gather.6
  563.6 186.7 all-gather.8
  752.0 22.5 all-gather.10
